TPU v7x, 128 devices: a whole 4x4x4 slice. The times are simulated.
128 devices in a mesh: tp: 8 (over z, x_hi), fsdp: 16 (over y, x_lo, core).
Axes of the slice: x: 4 (x_hi: 2, x_lo: 2; x = x_hi * 2 + x_lo), y: 4, z: 4, core: 2. Of those that a mesh axis runs over, the one named last changes fastest.
Arguments:
- t_hid: bfloat16 [8192, 16384], P('fsdp', 'tp'), may hold values from -400 to 400
- teacher_gain: float32 [16384], P('tp'), may hold values from 0.25 to 1.75
- proj: bfloat16 [16384, 4096], P('tp'), may hold values from -0.046875 to 0.046875
- owner: int32 [8192, 1], P('fsdp'), may hold values from 0 to 15; in each aligned block of 512 rows (0 to 511, 512 to 1023, ...) at most 48 rows name the same one
- seg_ids: int32 [16, 512], P('fsdp'), may hold values from 0 to 7, never falling along the last dimension, each value on 1 to 256 neighbouring positions
- student_ctx: bfloat16 [12288, 4096], P('fsdp'), may hold values from -6 to 6
- student_resid: bfloat16 [12288, 4096], P('fsdp', 'tp'), may hold values from -6 to 6
- w_out: bfloat16 [4096, 4096], P('fsdp', 'tp'), may hold values from -0.09375 to 0.09375
Outputs:
- loss: float32 [], replicated
- w_grad: bfloat16 [4096, 4096], P('fsdp', 'tp')
Inputs may be any that keep to these rules, and one draw needn't show every extreme that they name: Within each slab's 512 rows no owner is named by more than 48 rows, a bound that some block reaches of them.
All inputs are finite; a program needn't handle non-finite values.
Results may differ from a plain program's by a relative error of at most 0.0059.
Values may be sent and summed in bfloat16 or wider, within the bound.
A program may use at most 128 MiB of HBM per device.

v0:
```python
import jax
import jax.numpy as jnp
from jax import lax
from jax.sharding import PartitionSpec as P

D_T = 16384
D_S = 4096
SEGS = 8


def per_device(t_hid, teacher_gain, proj, owner, seg_ids, student_ctx, student_resid, w_out):
    slab = t_hid.shape[0]
    groups = lax.axis_size("fsdp")
    cap = 3 * slab // (2 * groups)
    width = student_resid.shape[1]
    wide = t_hid.astype(jnp.float32)
    squares = jnp.sum(wide * wide, axis=1)
    scaled = (wide * teacher_gain[None, :]).astype(jnp.bfloat16)
    raw = jnp.dot(scaled, proj, preferred_element_type=jnp.float32)
    summed, squares_all = lax.psum((raw, squares), "tp")
    mine = lax.dynamic_slice_in_dim(summed, lax.axis_index("tp") * width, width, 1)
    scale_rows = lax.rsqrt(squares_all / D_T + 1e-05)
    fitted = (mine * scale_rows[:, None]).astype(jnp.bfloat16)
    member = (seg_ids[0][:, None] == jnp.arange(SEGS, dtype=jnp.int32)[None, :]).astype(jnp.int32)
    counts = jnp.sum(member, axis=0)
    length = jnp.sum(member * counts[None, :], axis=1)
    weight = (1.0 / length.astype(jnp.float32)).astype(jnp.bfloat16)
    dest = owner[:, 0]
    marks = (dest[:, None] == jnp.arange(groups, dtype=jnp.int32)[None, :]).astype(jnp.int32)
    before = jnp.cumsum(marks, axis=0) - marks
    rank = jnp.sum(before * marks, axis=1)
    slot = dest * cap + rank
    buckets = jnp.zeros((groups * cap, width), jnp.bfloat16).at[slot].set(fitted)
    bucket_weight = jnp.zeros((groups * cap,), jnp.bfloat16).at[slot].set(weight)
    arrived, arrived_weight = (
        lax.all_to_all(buckets, "fsdp", split_axis=0, concat_axis=0, tiled=True),
        lax.all_to_all(bucket_weight, "fsdp", split_axis=0, concat_axis=0, tiled=True),
    )
    inputs = student_ctx
    projected = jnp.dot(
        inputs,
        lax.all_gather(w_out, "fsdp", axis=0, tiled=True),
        preferred_element_type=jnp.float32,
    )
    hidden = student_resid.astype(jnp.float32) + projected
    diff = hidden - arrived.astype(jnp.float32)
    weights = arrived_weight.astype(jnp.float32)
    denom = D_S * groups * SEGS
    local_loss = jnp.sum(weights * jnp.sum(diff * diff, axis=1))
    loss = lax.psum(local_loss, ("tp", "fsdp")) / denom
    grad_rows = (weights[:, None] * diff * (2.0 / denom)).astype(jnp.bfloat16)
    inputs = student_ctx
    w_grad = lax.psum_scatter(
        lax.dot_general(
            inputs, grad_rows, (((0,), (0,)), ((), ())), preferred_element_type=jnp.float32
        ),
        "fsdp",
        scatter_dimension=0,
        tiled=True,
    )
    return (loss, w_grad.astype(jnp.bfloat16))


def solution(mesh):
    return jax.shard_map(
        per_device,
        mesh=mesh,
        in_specs=(
            P("fsdp", "tp"),
            P("tp"),
            P("tp", None),
            P("fsdp", None),
            P("fsdp", None),
            P("fsdp", None),
            P("fsdp", "tp"),
            P("fsdp", "tp"),
        ),
        out_specs=(P(), P("fsdp", "tp")),
        check_vma=False,
    )
```

profile of v0, /device:TPU:1, one launch (start us, length us, event | category | flops | bytes accessed | tf_op | source)
XLA Modules:
  0.0 534.3 jit_solution(6365141898995217828)
XLA Ops:
  8.0 14.9 %fusion.2 = f32[512,4096]{1,0:T(8,128)} fusion(bf16[2048,4096]{1,0:T(8,128)(2,1)} %param.10, bf16[512,2048]{1,0:T(8,128)(2,1)} %param.8, f32[2048]{0:T(1024)} %param.9), kind=kOutput, calls=%fused_computation.7 | convolution fusion | flops 8593080320 | bytes 27271168 | tf_op jit(solution)/shard_map/dot_general | solution.py:19
  23.1 0.5 all-gather.2.cloned.1.call-update
  23.6 1.1 reduce-window.6
  24.8 0.2 slice_reduce_fusion
  25.4 3.8 scatter_custom_fusion
  29.2 0.7 all_to_all.16
  29.8 6.9 %all-to-all-start = ((bf16[16,48,1]{1,2,0:T(2,128)(2,1)}), bf16[16,48,1]{1,2,0:T(2,128)(2,1)S(1)}, u32[]{:S(2)}, u32[]{:S(2)}) async-start(bf16[16,48,1]{1,2,0:T(2,128)(2,1)} %all_to_all.16), calls=%async_computation | async-start | bytes 16384 | tf_op jit(solution)/shard_map/all_to_all | solution.py:37
  36.8 0.5 fusion.1
  37.3 22.9 %psum.22 = f32[512]{0:T(512)S(1)} all-reduce(f32[512]{0:T(512)S(1)} %fusion.1), channel_id=1, replica_groups=mesh['tp'=8,'fsdp'=16] {'tp'}, use_global_device_ids=true, to_apply=%region_8.9 | all-reduce | flops 512 | bytes 4096 | tf_op jit(solution)/shard_map/psum | solution.py:20
  60.1 327.9 %all-reduce.2.cloned.1.call-done = f32[512,4096]{1,0:T(8,128)} async-done(((f32[512,4096]{1,0:T(8,128)}), f32[512,4096]{1,0:T(8,128)}) %all-reduce.2.cloned.1.call-update) | async-done | bytes 8388624 | tf_op jit(solution)/shard_map/psum | solution.py:20
  388.1 4.1 scatter_custom_fusion.1
  392.2 5.0 all-to-all-start.1
  397.1 0.2 reduce-scatter.2.cloned.1.call-start
  397.4 1.2 copy.25
  398.6 11.5 %all-to-all-done.1 = bf16[16,48,512]{2,1,0:T(8,128)(2,1)S(1)} async-done(((bf16[16,48,512]{2,1,0:T(8,128)(2,1)}), bf16[16,48,512]{2,1,0:T(8,128)(2,1)S(1)}, u32[]{:S(2)}, u32[]{:S(2)}) %all-to-all-start.1) | async-done | bytes 786464 | tf_op jit(solution)/shard_map/all_to_all | solution.py:36
  410.1 0.2 bitcast_convert_fusion
  410.4 0.5 copy.26
  410.9 7.9 %multiply_reduce_fusion = (f32[768]{0:T(1024)S(1)}, f32[768,512]{0,1:T(8,128)S(1)}) fusion(f32[768,512]{0,1:T(8,128)S(1)} %copy.26, bf16[768,4096]{1,0:T(8,128)(2,1)} %param.13, bf16[4096,512]{1,0:T(8,128)(2,1)} %all-gather.2.cloned.1.call-done, bf16[768,512]{0,1:T(8,128)(2,1)} %copy.25), kind=kOutput, calls=%fused_computation.10 | convolution fusion | flops 3223190784 | bytes 14420992 | tf_op jit(solution)/shard_map/dot_general | solution.py:40
  418.8 8.4 %convolution_bitcast_fusion = f32[4096,512]{0,1:T(8,128)} fusion(bf16[768,4096]{1,0:T(8,128)(2,1)} %param.13, f32[768,512]{0,1:T(8,128)S(1)} %get-tuple-element.11, f32[768]{0:T(1024)S(1)} %reshape.41), kind=kOutput, calls=%fused_computation.2 | convolution fusion | flops 3222405120 | bytes 16256000 | tf_op jit(solution)/shard_map/dot_general | solution.py:54
  427.3 0.6 multiply_reduce_fusion.1
  427.9 65.4 %psum.23 = f32[]{:T(128)} all-reduce(f32[]{:T(128)} %multiply_reduce_fusion.1), channel_id=1, replica_groups=mesh['tp'=8,'fsdp'=16] {'tp','fsdp'}, use_global_device_ids=true, to_apply=%region_12.13 | all-reduce | flops 1 | bytes 8 | tf_op jit(solution)/shard_map/psum | solution.py:50
  494.0 29.9 %reduce-scatter.2.cloned.1.call-done = f32[256,512]{0,1:T(8,128)} async-done(((f32[4096,512]{0,1:T(8,128)}), f32[256,512]{0,1:T(8,128)}) %reduce-scatter.2.cloned.1.call-update) | async-done | bytes 524304 | tf_op jit(solution)/shard_map/reduce_scatter | solution.py:53
  523.8 1.1 convert_element_type.68
  524.9 0.8 copy.27
  (26 shorter events, 0.7 us)
Async XLA Ops:
  8.0 380.1 %all-reduce.2.cloned.1.call-start = ((), (), s32[]{:S(2)}) async-start(), calls=%async_computation.4 | async-start | bytes 16777216 | tf_op jit(solution)/shard_map/psum | solution.py:20
  23.0 0.7 copy-start.2
  23.0 2.1 copy-start.3
  23.0 13.8 %copy-start = (bf16[512,2048]{1,0:T(8,128)(2,1)S(1)}, bf16[512,2048]{1,0:T(8,128)(2,1)}, u32[]{:S(2)}) copy-start(bf16[512,2048]{1,0:T(8,128)(2,1)} %param.8) | copy-start | bytes 6291460
  23.0 374.4 %copy-start.1 = (bf16[768,512]{1,0:T(8,128)(2,1)S(1)}, bf16[768,512]{1,0:T(8,128)(2,1)}, u32[]{:S(2)}) copy-start(bf16[768,512]{1,0:T(8,128)(2,1)} %param.14) | copy-start | bytes 2359300
  23.0 387.9 %all-gather.2.cloned.1.call-start = ((), (), s32[]{:S(2)}) async-start(), calls=%async_computation.3 | async-start | bytes 4456448 | tf_op jit(solution)/shard_map/all_gather | solution.py:42
  29.8 362.3 %all-to-all-start = ((bf16[16,48,1]{1,2,0:T(2,128)(2,1)}), bf16[16,48,1]{1,2,0:T(2,128)(2,1)S(1)}, u32[]{:S(2)}, u32[]{:S(2)}) async-start(bf16[16,48,1]{1,2,0:T(2,128)(2,1)} %all_to_all.16), calls=%async_computation | async-start | bytes 16384 | tf_op jit(solution)/shard_map/all_to_all | solution.py:37
  392.2 18.0 %all-to-all-start.1 = ((bf16[16,48,512]{2,1,0:T(8,128)(2,1)}), bf16[16,48,512]{2,1,0:T(8,128)(2,1)S(1)}, u32[]{:S(2)}, u32[]{:S(2)}) async-start(bf16[16,48,512]{2,1,0:T(8,128)(2,1)} %bitcast.6), calls=%async_computation.1 | async-start | bytes 1572864 | tf_op jit(solution)/shard_map/all_to_all | solution.py:36
  397.1 126.7 %reduce-scatter.2.cloned.1.call-start = ((), (), s32[]{:S(2)}) async-start(), calls=%async_computation.5 | async-start | bytes 8912896 | tf_op jit(solution)/shard_map/reduce_scatter | solution.py:53
Sparse Core Ops, SparseCore 0:
  23.1 364.8 all-reduce.1
Sparse Core Ops, SparseCore 1:
  25.2 163.3 all-gather.1
  427.3 96.5 reduce-scatter.1
where the time goes:
time: 535 us; the launch traced here: 534 us
  waiting for transfers between devices  370 us (69%)
  blocking collectives  88.3 us (17%)
  matrix products  31.2 us (6%)
  between operations  17.4 us (3%)
  starting transfers between devices  12.2 us (2%)
  other arithmetic  8.02 us (1%)
  local copies, waits for them, and re-layouts  7.38 us (1%)
    psum x1, waiting for transfers between devices, per_device(): summed, squares_all = lax.psum((raw, squares), 'tp')  328 us
    psum x1, blocking collectives, per_device(): loss = lax.psum(local_loss, ('tp', 'fsdp')) / denom  65.4 us
    reduce_scatter x1, waiting for transfers between devices, per_device(): lax.psum_scatter(lax.dot_general(inputs, grad_rows, (((0,), (0,)), ((), (...  29.9 us
    psum x1, blocking collectives, per_device(): summed, squares_all = lax.psum((raw, squares), 'tp')  22.9 us
    dot_general x1, matrix products, per_device(): raw = jnp.dot(scaled, proj, preferred_element_type=jnp.float32)  14.9 us
    all_to_all x1, waiting for transfers between devices, per_device(): lax.all_to_all(buckets, 'fsdp', split_axis=0, concat_axis=0, tiled=True)  11.5 us
  transfers between devices with their start and end apart: 5, of which 3 were waited for; matrix products, arithmetic and copies ran while one was open for 2% of the time, Pallas kernels for 0%

commit v1 on v0

v1 whole, which is shorter than its diff:
```python
import jax
import jax.numpy as jnp
from jax import lax
from jax.experimental import pallas as pl
from jax.experimental.pallas import tpu as pltpu
from jax.sharding import PartitionSpec as P

D_T = 16384
D_S = 4096
SEGS = 8
TP = 8
FS = 16
SLAB = 512
KT = D_T // TP
COLS = D_S // TP
CAP = 48
ROWS = FS * CAP
KB = D_S // FS
HALF = COLS // 2
LANES = 128
DENOM = D_S * FS * SEGS
F32 = jnp.float32
BF16 = jnp.bfloat16
MESH = pl.DeviceIdType.MESH


def kernel(t_ref, gain_ref, proj_ref, own_ref, seg_ref, ctx_ref, resid_ref, wout_ref,
           out_ref, loss_ref,
           tv, sc, pv, cv, rv, wv, part, zr2, zr1, xr, sq, scale, onehot, buckets, bw, arr, wts,
           hv, gv, gt, pg, rsv, lb, lt,
           ld_sem, pv_sem, core_s, core_r, wo_s, wo_r, wt_s, wt_r, sq_s, sq_r,
           z2_s, z2_r, z1_s, z1_r, xh_s, xh_r, ar_s, ar_r, rs_s, rs_r, l1_s, l1_r, l2_s, l2_r, my_sem):
    t = lax.axis_index("tp")
    f = lax.axis_index("fsdp")
    z, xh = t // 2, t % 2
    g, c = f // 2, f % 2

    def tp_dev(i):
        return (i, f)

    def fs_dev(i):
        return (t, i)

    def rcopy(src, dst, ss, rs, dev):
        return pltpu.make_async_remote_copy(src_ref=src, dst_ref=dst, send_sem=ss, recv_sem=rs,
                                            device_id=dev, device_id_type=MESH)

    z_up, z_dn = lax.rem(t + 2, TP), lax.rem(t + 6, TP)
    xh_peer = t + 1 - 2 * xh
    core_peer = f + 1 - 2 * c

    ld_t = pltpu.make_async_copy(t_ref, tv, ld_sem.at[0])
    ld_t.start()
    rels = (2, 1, 3, 0)

    def unit_copy(q, r, x):
        dest = lax.rem(z + rels[r], 4) * 2 + x
        col = pl.multiple_of(dest * COLS + q * HALF, HALF)
        u = (q * 4 + r) * 2 + x
        return pltpu.make_async_copy(proj_ref.at[:, pl.ds(col, HALF)], pv.at[u], pv_sem.at[u])

    for q in range(2):
        for r in range(4):
            for x in range(2):
                unit_copy(q, r, x).start()
    my_rows = pl.ds(pl.multiple_of(c * ROWS, ROWS), ROWS)
    ld_c = pltpu.make_async_copy(ctx_ref, cv.at[my_rows], ld_sem.at[1])
    ld_c.start()
    ld_r, ld_w = [], []
    for q in range(2):
        mine = pl.ds(pl.multiple_of(q * HALF + c * LANES, LANES), LANES)
        ld_r.append(pltpu.make_async_copy(resid_ref.at[:, mine], rv.at[q, my_rows], ld_sem.at[2 + q]))
        ld_w.append(pltpu.make_async_copy(
            wout_ref.at[:, mine], wv.at[pl.ds(pl.multiple_of(f * KB, KB), KB), pl.ds(q * LANES, LANES)],
            ld_sem.at[4 + q]))
    for cp in ld_r + ld_w:
        cp.start()

    barrier = pltpu.get_barrier_semaphore()

    def greet_fs(s, _):
        pl.semaphore_signal(barrier, inc=1, device_id=fs_dev(lax.rem(f + s, FS)), device_id_type=MESH)
        return 0

    def greet_tp(s, _):
        pl.semaphore_signal(barrier, inc=1, device_id=tp_dev(lax.rem(t + s, TP)), device_id_type=MESH)
        return 0

    lax.fori_loop(1, FS, greet_fs, 0)
    lax.fori_loop(1, TP, greet_tp, 0)

    own = own_ref[...]
    seg = seg_ref[...]
    marks = (lax.broadcasted_iota(jnp.int32, (FS, SLAB), 0) == own)
    earlier = (lax.broadcasted_iota(jnp.int32, (SLAB, SLAB), 0)
               < lax.broadcasted_iota(jnp.int32, (SLAB, SLAB), 1)).astype(F32).astype(BF16)
    marks = marks.astype(F32)
    before = jnp.dot(marks.astype(BF16), earlier, preferred_element_type=F32)
    rank = jnp.sum(before * marks, axis=0, keepdims=True).astype(jnp.int32)
    slot = own * CAP + rank
    onehot[...] = (lax.broadcasted_iota(jnp.int32, (ROWS, SLAB), 0) == slot).astype(F32).astype(BF16)
    member = (lax.broadcasted_iota(jnp.int32, (SEGS, SLAB), 0) == seg).astype(F32)
    counts = jnp.sum(member, axis=1, keepdims=True)
    length = jnp.sum(member * counts, axis=0, keepdims=True)
    weight = (1.0 / length).astype(BF16)
    bw[...] = lax.dot_general(onehot[...], jnp.broadcast_to(weight, (LANES, SLAB)), (((1,), (1,)), ((), ())),
                              preferred_element_type=F32).astype(BF16)

    ld_t.wait()

    def scale_step(i, _):
        rows = pl.ds(pl.multiple_of(i * 64, 64), 64)
        wide = tv[rows, :].astype(F32)
        sc[rows, :] = (wide * gain_ref[...]).astype(BF16)
        two = wide * wide
        acc = two[:, 0:LANES]
        for k in range(1, KT // LANES):
            acc = acc + two[:, k * LANES:(k + 1) * LANES]
        scale[rows, :] = acc
        return 0

    lax.fori_loop(0, SLAB // 64, scale_step, 0)
    sq[t] = jnp.broadcast_to(jnp.sum(scale[...].T, axis=0, keepdims=True), (8, SLAB))

    pl.semaphore_wait(barrier, FS - 1 + TP - 1)

    other = 1 - c
    cx = [rcopy(ctx_ref, cv.at[my_rows], core_s.at[0], core_r.at[0], fs_dev(core_peer))]
    for q in range(2):
        theirs = pl.ds(pl.multiple_of(q * HALF + other * LANES, LANES), LANES)
        cx.append(rcopy(resid_ref.at[:, theirs], rv.at[q, my_rows], core_s.at[1 + q], core_r.at[1 + q], fs_dev(core_peer)))

    def wo_copy(q, src, dst):
        lanes = pl.ds(pl.multiple_of(q * HALF + (dst % 2) * LANES, LANES), LANES)
        return rcopy(wout_ref.at[:, lanes],
                     wv.at[pl.ds(pl.multiple_of(src * KB, KB), KB), pl.ds(q * LANES, LANES)],
                     wo_s.at[q, dst], wo_r.at[q, src], fs_dev(dst))

    def wt_copy(src, dst):
        return rcopy(bw.at[pl.ds(pl.multiple_of((dst // 2) * 2 * CAP, 2 * CAP), 2 * CAP)], wts.at[src],
                     wt_s.at[dst], wt_r.at[src], fs_dev(dst))

    def sq_copy(src, dst):
        return rcopy(sq.at[src], sq.at[src], sq_s.at[dst], sq_r.at[src], tp_dev(dst))

    def each_fs(fn):
        def body(s, _):
            fn(lax.rem(f + s, FS))
            return 0
        lax.fori_loop(1, FS, body, 0)

    def each_tp(fn):
        def body(s, _):
            fn(lax.rem(t + s, TP))
            return 0
        lax.fori_loop(1, TP, body, 0)

    each_tp(lambda d: sq_copy(t, d).start())
    wt_mine = pltpu.make_async_copy(bw.at[pl.ds(pl.multiple_of(g * 2 * CAP, 2 * CAP), 2 * CAP)], wts.at[f], my_sem.at[0])
    wt_mine.start()

    def z2_copy(q, up):
        return rcopy(part.at[(q * 4 + 0) * 2 + up], zr2.at[q, up], z2_s.at[q, up], z2_r.at[q, up],
                     tp_dev(z_up if up else z_dn))

    def z1_copy(q, up, x):
        return rcopy(part.at[(q * 4 + (1 if up else 2)) * 2 + x], zr1.at[q, up, x],
                     z1_s.at[q, up, x], z1_r.at[q, up, x], tp_dev(z_up if up else z_dn))

    def product(q, r):
        for x in range(2):
            unit_copy(q, r, x).wait()

        def body(x, _):
            u = (q * 4 + r) * 2 + x
            part[u] = jnp.dot(sc[...], pv[u], preferred_element_type=F32).astype(BF16)
            return 0

        lax.fori_loop(0, 2, body, 0)

    def teacher_sends(q, r):
        if r == 0:
            z2_copy(q, 1).start()
            z2_copy(q, 0).start()
        elif r == 1:
            z1_copy(q, 1, 0).start()
        elif r == 2:
            z1_copy(q, 0, 1).start()

    def z_middle(q):
        for up in (1, 0):
            z2_copy(q, up).wait_recv()
            u = (q * 4 + (1 if up else 2)) * 2 + up
            part[u] = (part[u].astype(F32) + zr2[q, up].astype(F32)).astype(BF16)
            z1_copy(q, up, up).start()

    def z_last(q):
        for up in (1, 0):
            for x in range(2):
                z1_copy(q, up, x).wait_recv()

    def z_total(q, x):
        return (part[(q * 4 + 3) * 2 + x].astype(F32) + zr1[q, 0, x].astype(F32)) + zr1[q, 1, x].astype(F32)

    def xh_copy(q):
        return rcopy(part.at[(q * 4 + 3) * 2 + (1 - xh)], xr.at[q], xh_s.at[q], xh_r.at[q], tp_dev(xh_peer))

    def x_send(q):
        part[(q * 4 + 3) * 2 + (1 - xh)] = z_total(q, 1 - xh).astype(BF16)
        xh_copy(q).start()

    def ar_copy(q, src, dst):
        return rcopy(buckets.at[q, dst % 2, pl.ds(pl.multiple_of((dst // 2) * 2 * CAP, 2 * CAP), 2 * CAP)],
                     arr.at[q, src], ar_s.at[q, dst], ar_r.at[q, src], fs_dev(dst))

    def ar_mine(q):
        return pltpu.make_async_copy(
            buckets.at[q, c, pl.ds(pl.multiple_of(g * 2 * CAP, 2 * CAP), 2 * CAP)], arr.at[q, f], my_sem.at[1 + q])

    def regroup(q):
        xh_copy(q).wait_recv()
        raw = z_total(q, xh) + xr[q].astype(F32)
        by = scale[...]
        fitted = (raw * jnp.concatenate([by, by], axis=1)).astype(BF16)
        moved = jnp.dot(onehot[...], fitted, preferred_element_type=F32).astype(BF16)
        buckets[q, 0] = moved[:, :LANES]
        buckets[q, 1] = moved[:, LANES:]
        each_fs(lambda d: ar_copy(q, f, d).start())
        ar_mine(q).start()

    def rs_copy(q, src, dst):
        return rcopy(pg.at[q, dst], rsv.at[q, src], rs_s.at[q, dst], rs_r.at[q, src], fs_dev(dst))

    def rs_mine(q):
        return pltpu.make_async_copy(pg.at[q, f], rsv.at[q, f], my_sem.at[3 + q])

    def gradient(q, total):
        ar_mine(q).wait()

        def one(s, total):
            src = lax.rem(f + s, FS)

            @pl.when(s > 0)
            def _():
                ar_copy(q, src, f).wait_recv()

            for j in range(2):
                rows = pl.ds(pl.multiple_of(j * ROWS + src * CAP, CAP), CAP)
                diff = hv[rows, q * LANES:(q + 1) * LANES] - arr[q, src, j * CAP:(j + 1) * CAP, :].astype(F32)
                wd = wts[src, j * CAP:(j + 1) * CAP, :].astype(F32) * diff
                gv[rows, :] = wd * (2.0 / DENOM)
                terms = wd * diff
                for k in range(CAP // 8):
                    total = total + terms[k * 8:(k + 1) * 8]
            return total

        total = lax.fori_loop(0, FS, one, total)
        gt[...] = gv[...].T.astype(BF16)

        def term(i, _):
            dst = lax.rem(f + 1 + i, FS)
            cols = pl.ds(pl.multiple_of(dst * KB, KB), KB)
            pg[q, dst] = jnp.dot(gt[...], cv[:, cols], preferred_element_type=F32).astype(BF16)

            @pl.when(i < FS - 1)
            def _():
                rs_copy(q, f, dst).start()

            return 0

        lax.fori_loop(0, FS, term, 0)
        rs_mine(q).start()
        return total

    def collect(q):
        each_fs(lambda s: rs_copy(q, s, f).wait_recv())
        rs_mine(q).wait()
        for k in range(2):
            acc = rsv[q, k].astype(F32)
            for i in range(1, FS // 2):
                acc = acc + rsv[q, 2 * i + k].astype(F32)
            out_ref[q * HALF + k * LANES:q * HALF + (k + 1) * LANES, :] = acc.astype(BF16)

    for r in range(4):
        product(0, r)
        teacher_sends(0, r)
        if r == 0:
            for cp in cx:
                cp.start()
            each_fs(lambda d: wo_copy(0, f, d).start())
            each_fs(lambda d: wo_copy(1, f, d).start())
            each_fs(lambda d: wt_copy(f, d).start())
    z_middle(0)
    for r in range(4):
        product(1, r)
        teacher_sends(1, r)

    each_tp(lambda s: sq_copy(s, t).wait_recv())
    squares = sq[0]
    for i in range(1, TP):
        squares = squares + sq[i]
    rows_scale = lax.rsqrt(squares[0:1] / D_T + 1e-05)
    scale[...] = jnp.broadcast_to(rows_scale, (LANES, SLAB)).T

    z_middle(1)

    ld_c.wait()
    for cp in ld_r + ld_w:
        cp.wait()
    for cp in cx:
        cp.wait_recv()
    each_fs(lambda s: wo_copy(0, s, f).wait_recv())
    each_fs(lambda s: wo_copy(1, s, f).wait_recv())

    def hidden_step(i, _):
        rows = pl.ds(pl.multiple_of(i * 256, 256), 256)
        prod = jnp.dot(cv[rows, :], wv[...], preferred_element_type=F32)
        hv[rows, :] = prod + jnp.concatenate([rv[0, rows, :].astype(F32), rv[1, rows, :].astype(F32)], axis=1)
        return 0

    lax.fori_loop(0, 2 * ROWS // 256, hidden_step, 0)

    z_last(0)
    x_send(0)
    regroup(0)
    z_last(1)
    x_send(1)
    each_fs(lambda s: wt_copy(s, f).wait_recv())
    wt_mine.wait()
    total = gradient(0, jnp.zeros((8, LANES), F32))
    regroup(1)
    total = gradient(1, total)

    def l1_copy(src, dst):
        return rcopy(lb.at[src], lb.at[src], l1_s.at[dst], l1_r.at[src], fs_dev(dst))

    def l2_copy(src, dst):
        return rcopy(lt.at[src], lt.at[src], l2_s.at[dst], l2_r.at[src], tp_dev(dst))

    lb[f] = total
    each_fs(lambda d: l1_copy(f, d).start())
    collect(0)
    each_fs(lambda s: l1_copy(s, f).wait_recv())
    total = lb[0]
    for i in range(1, FS):
        total = total + lb[i]
    lt[t] = total
    each_tp(lambda d: l2_copy(t, d).start())
    collect(1)
    each_tp(lambda s: l2_copy(s, t).wait_recv())
    total = lt[0]
    for i in range(1, TP):
        total = total + lt[i]
    total = jnp.sum(jnp.sum(total, axis=0, keepdims=True), axis=1, keepdims=True) / DENOM
    loss_ref[...] = jnp.broadcast_to(total, (8, LANES))

    for cp in cx:
        cp.wait_send()
    for q in range(2):
        for up in range(2):
            z2_copy(q, up).wait_send()
            for x in range(2):
                z1_copy(q, up, x).wait_send()
        xh_copy(q).wait_send()

    def drain_fs(d):
        for q in range(2):
            wo_copy(q, f, d).wait_send()
            ar_copy(q, f, d).wait_send()
            rs_copy(q, f, d).wait_send()
        wt_copy(f, d).wait_send()
        l1_copy(f, d).wait_send()

    def drain_tp(d):
        sq_copy(t, d).wait_send()
        l2_copy(t, d).wait_send()

    each_fs(drain_fs)
    each_tp(drain_tp)


def per_device(t_hid, teacher_gain, proj, owner, seg_ids, student_ctx, student_resid, w_out):
    dma = pltpu.SemaphoreType.DMA
    anyspace = pl.BlockSpec(memory_space=pl.ANY)
    vmem = pl.BlockSpec(memory_space=pltpu.VMEM)
    out, loss = pl.pallas_call(
        kernel,
        out_shape=(jax.ShapeDtypeStruct((COLS, KB), BF16), jax.ShapeDtypeStruct((8, LANES), F32)),
        in_specs=[anyspace, vmem, anyspace, vmem, vmem, anyspace, anyspace, anyspace],
        out_specs=(vmem, vmem),
        scratch_shapes=[
            pltpu.VMEM((SLAB, KT), BF16),
            pltpu.VMEM((SLAB, KT), BF16),
            pltpu.VMEM((16, KT, HALF), BF16),
            pltpu.VMEM((2 * ROWS, D_S), BF16),
            pltpu.VMEM((2, 2 * ROWS, LANES), BF16),
            pltpu.VMEM((D_S, HALF), BF16),
            pltpu.VMEM((16, SLAB, HALF), BF16),
            pltpu.VMEM((2, 2, SLAB, HALF), BF16),
            pltpu.VMEM((2, 2, 2, SLAB, HALF), BF16),
            pltpu.VMEM((2, SLAB, HALF), BF16),
            pltpu.VMEM((TP, 8, SLAB), F32),
            pltpu.VMEM((SLAB, LANES), F32),
            pltpu.VMEM((ROWS, SLAB), BF16),
            pltpu.VMEM((2, 2, ROWS, LANES), BF16),
            pltpu.VMEM((ROWS, LANES), BF16),
            pltpu.VMEM((2, FS, 2 * CAP, LANES), BF16),
            pltpu.VMEM((FS, 2 * CAP, LANES), BF16),
            pltpu.VMEM((2 * ROWS, HALF), F32),
            pltpu.VMEM((2 * ROWS, LANES), F32),
            pltpu.VMEM((LANES, 2 * ROWS), BF16),
            pltpu.VMEM((2, FS, LANES, KB), BF16),
            pltpu.VMEM((2, FS, LANES, KB), BF16),
            pltpu.VMEM((FS, 8, LANES), F32),
            pltpu.VMEM((TP, 8, LANES), F32),
            dma((8,)), dma((16,)), dma((3,)), dma((3,)),
            dma((2, FS)), dma((2, FS)), dma((FS,)), dma((FS,)), dma((TP,)), dma((TP,)),
            dma((2, 2)), dma((2, 2)), dma((2, 2, 2)), dma((2, 2, 2)), dma((2,)), dma((2,)),
            dma((2, FS)), dma((2, FS)), dma((2, FS)), dma((2, FS)),
            dma((FS,)), dma((FS,)), dma((TP,)), dma((TP,)), dma((5,)),
        ],
        compiler_params=pltpu.CompilerParams(collective_id=0, has_side_effects=True, vmem_limit_bytes=62 << 20),
        cost_estimate=pl.CostEstimate(flops=15 * 10 ** 9, bytes_accessed=32 << 20, transcendentals=0),
    )(t_hid, teacher_gain.reshape(1, KT), proj, owner.reshape(1, SLAB), seg_ids, student_ctx, student_resid, w_out)
    return loss[0, 0], out.T


def solution(mesh):
    return jax.shard_map(
        per_device,
        mesh=mesh,
        in_specs=(
            P("fsdp", "tp"),
            P("tp"),
            P("tp", None),
            P("fsdp", None),
            P("fsdp", None),
            P("fsdp", None),
            P("fsdp", "tp"),
            P("fsdp", "tp"),
        ),
        out_specs=(P(), P("fsdp", "tp")),
        check_vma=False,
    )
```

time: 535 us -> 108 us (0.20)
  waiting for transfers between devices: 370 us -> 0 us
  Pallas kernels: 0 us -> 105 us
  blocking collectives: 88.3 us -> 0 us
  matrix products: 31.2 us -> 0 us
  between operations: 17.4 us -> 0.64 us
  starting transfers between devices: 12.2 us -> 0 us
  other arithmetic: 8.02 us -> 0 us
    psum x1 -> x0, waiting for transfers between devices: 328 us -> none  [per_device(): summed, squares_all = lax.psum((raw, squares), 'tp')]
    pallas_call x0 -> x1, Pallas kernels: none -> 105 us  [per_device(): pl.pallas_call(kernel, out_shape=(jax.ShapeDtypeStruct((COLS, KB), BF16),...]
    psum x2 -> x0, blocking collectives: 88.3 us -> none  [the longest x1 65.4 us: per_device(): loss = lax.psum(local_loss, ('tp', 'fsdp')) / denom]
    dot_general x3 -> x0, matrix products: 31.2 us -> none  [the longest x1 14.9 us: per_device(): raw = jnp.dot(scaled, proj, preferred_element_type=jnp.float32)]
    reduce_scatter x1 -> x0, waiting for transfers between devices: 29.9 us -> none  [per_device(): lax.psum_scatter(lax.dot_general(inputs, grad_rows, (((0,), (0,)), ((), (...]
    all_to_all x2 -> x0, starting transfers between devices: 11.9 us -> none  [the longest x1 6.91 us: per_device(): lax.all_to_all(bucket_weight, 'fsdp', split_axis=0, concat_axis=0, tiled=...]
    all_to_all x2 -> x0, waiting for transfers between devices: 11.5 us -> none  [the longest x1 11.5 us: per_device(): lax.all_to_all(buckets, 'fsdp', split_axis=0, concat_axis=0, tiled=True)]
  transfers between devices with their start and end apart: 5 -> 0, of which waited for: 3 -> 0; matrix products, arithmetic and copies ran while one was open for 2% -> 0% of each run, Pallas kernels for 0% -> 0%
where the time goes in v1:
time: 108 us
  Pallas kernels  105 us (97%)
  local copies, waits for them, and re-layouts  2.99 us (3%)
    pallas_call x1, Pallas kernels, per_device(): pl.pallas_call(kernel, out_shape=(jax.ShapeDtypeStruct((COLS, KB), BF16),...  105 us

profile of v1, /device:TPU:1, one launch (start us, length us, event | category | flops | bytes accessed | tf_op | source)
XLA Modules:
  0.0 108.3 jit_solution(16817988628849265414)
XLA Ops:
  0.6 104.6 %shard_map.95 = (bf16[512,256]{1,0:T(8,128)(2,1)}, f32[8,128]{1,0:T(8,128)}) custom-call(bf16[512,2048]{1,0:T(8,128)(2,1)} %t_ref.1, f32[1,2048]{1,0:T(1,128)} %bitcast.5, bf16[2048,4096]{1,0:T(8,128)(2,1)} %proj_ref.1, s32[1,512]{1,0:T(1,128)} %bitcast.6, s32[1,512]{1,0:T(1,128)} %seg_ref.1, bf16[768,4096]{1,0:T(8,128)(2,1)} %ctx_ref.1, ...), custom_call_target="tpu_custom_call" | custom-call | flops 15000000512 | bytes 33554432 | tf_op jit(solution)/shard_map/pallas_call | solution.py:386
  105.3 1.2 %slice.3 = f32[1,1]{1,0:T(1,128)} slice(f32[8,128]{1,0:T(8,128)} %get-tuple-element.4), slice={[0:1], [0:1]} | slice | bytes 8 | tf_op jit(solution)/shard_map/slice | solution.py:425
  106.5 1.8 %copy.10 = bf16[256,512]{1,0:T(8,128)(2,1)} copy(bf16[256,512]{0,1:T(8,128)(2,1)} %bitcast.4) | data formatting | bytes 524288

commit v2 on v0

v2 whole, which is shorter than its diff:
```python
import jax
import jax.numpy as jnp
from jax import lax
from jax.experimental import pallas as pl
from jax.experimental.pallas import tpu as pltpu
from jax.sharding import PartitionSpec as P

D_T = 16384
D_S = 4096
SEGS = 8
TP = 8
FS = 16
SLAB = 512
KT = D_T // TP
COLS = D_S // TP
CAP = 48
ROWS = FS * CAP
KB = D_S // FS
HALF = COLS // 2
LANES = 128
DENOM = D_S * FS * SEGS
F32 = jnp.float32
BF16 = jnp.bfloat16
MESH = pl.DeviceIdType.MESH


def kernel(t_ref, gain_ref, proj_ref, own_ref, seg_ref, ctx_ref, resid_ref, wout_ref,
           out_ref, loss_ref,
           tv, sc, pv, cv, rv, wv, part, zr2, zr1, xr, sq, scale, onehot, buckets, bw, arr, wts, wcol,
           hv, gv, gt, pg, rsv, rsy, lb, lt,
           ld_sem, pv_sem, my_sem, core_s, core_r, w_s, wo_r, wy_r, wf_r, wg_r, wx_r, wt_s, wt_r, sq_s, sq_r,
           z_s, z2_r, z1_r, xh_r, ar_s, ar_r, rs_s, rs_r, ry_s, ry_r, l1_s, l1_r, l2_s, l2_r):
    t = lax.axis_index("tp")
    f = lax.axis_index("fsdp")
    z, xh = t // 2, t % 2
    g, c = f // 2, f % 2

    def tp_dev(i):
        return (i, f)

    def fs_dev(i):
        return (t, i)

    def rcopy(src, dst, ss, rs, dev):
        return pltpu.make_async_remote_copy(src_ref=src, dst_ref=dst, send_sem=ss, recv_sem=rs,
                                            device_id=dev, device_id_type=MESH)

    def arrived(view, sem):
        rcopy(view, view, sem, sem, fs_dev(core_peer)).wait_recv()

    def sent(view, sem):
        rcopy(view, view, sem, sem, fs_dev(core_peer)).wait_send()

    z_up, z_dn = lax.rem(t + 2, TP), lax.rem(t + 6, TP)
    xh_peer = t + 1 - 2 * xh
    core_peer = f + 1 - 2 * c
    y, xl = f // 4, g % 2
    xl_chip = g + 1 - 2 * xl

    barrier = pltpu.get_barrier_semaphore()

    def greet_fs(s, _):
        pl.semaphore_signal(barrier, inc=1, device_id=fs_dev(lax.rem(f + s, FS)), device_id_type=MESH)
        return 0

    def greet_tp(s, _):
        pl.semaphore_signal(barrier, inc=1, device_id=tp_dev(lax.rem(t + s, TP)), device_id_type=MESH)
        return 0

    lax.fori_loop(1, FS, greet_fs, 0)
    lax.fori_loop(1, TP, greet_tp, 0)

    ld_t = pltpu.make_async_copy(t_ref, tv, ld_sem.at[0])
    ld_t.start()
    rels = (2, 1, 3, 0)

    def unit_copy(q, r, x):
        dest = lax.rem(z + rels[r], 4) * 2 + x
        col = pl.multiple_of(dest * COLS + q * HALF, HALF)
        u = (q * 4 + r) * 2 + x
        return pltpu.make_async_copy(proj_ref.at[:, pl.ds(col, HALF)], pv.at[u], pv_sem.at[q * 4 + r])

    for x in range(2):
        unit_copy(0, 0, x).start()
    my_rows = pl.ds(pl.multiple_of(c * ROWS, ROWS), ROWS)
    ld_c = pltpu.make_async_copy(ctx_ref, cv.at[my_rows], ld_sem.at[1])
    ld_r, ld_w = [], []
    for q in range(2):
        mine = pl.ds(pl.multiple_of(q * HALF + c * LANES, LANES), LANES)
        ld_r.append(pltpu.make_async_copy(resid_ref.at[:, mine], rv.at[q, my_rows], ld_sem.at[2 + q]))
        ld_w.append(pltpu.make_async_copy(
            wout_ref.at[:, mine], wv.at[pl.ds(pl.multiple_of(f * KB, KB), KB), pl.ds(q * LANES, LANES)],
            ld_sem.at[4 + q]))
    own = own_ref[...]
    seg = seg_ref[...]
    marks = (lax.broadcasted_iota(jnp.int32, (FS, SLAB), 0) == own)
    earlier = (lax.broadcasted_iota(jnp.int32, (SLAB, SLAB), 0)
               < lax.broadcasted_iota(jnp.int32, (SLAB, SLAB), 1)).astype(F32).astype(BF16)
    marks = marks.astype(F32)
    before = jnp.dot(marks.astype(BF16), earlier, preferred_element_type=F32)
    rank = jnp.sum(before * marks, axis=0, keepdims=True).astype(jnp.int32)
    slot = own * CAP + rank
    onehot[...] = (lax.broadcasted_iota(jnp.int32, (ROWS, SLAB), 0) == slot).astype(F32).astype(BF16)
    member = (lax.broadcasted_iota(jnp.int32, (SEGS, SLAB), 0) == seg).astype(F32)
    counts = jnp.sum(member, axis=1, keepdims=True)
    length = jnp.sum(member * counts, axis=0, keepdims=True)
    weight = jnp.broadcast_to((1.0 / length).astype(BF16), (16, SLAB))
    wide_slot = (own // 2) * LANES + (own % 2) * CAP + rank
    spread = (lax.broadcasted_iota(jnp.int32, (FS // 2 * LANES, SLAB), 0) == wide_slot).astype(F32).astype(BF16)
    moved = lax.dot_general(weight, spread, (((1,), (1,)), ((), ())), preferred_element_type=F32)
    for i in range(FS // 2):
        bw[i] = moved[0:8, i * LANES:(i + 1) * LANES]

    ld_t.wait()
    for q in range(2):
        for r in range(4):
            for x in range(2):
                if q or r:
                    unit_copy(q, r, x).start()
    for cp in ld_w + ld_r + [ld_c]:
        cp.start()

    def scale_step(i, _):
        rows = pl.ds(pl.multiple_of(i * 64, 64), 64)
        wide = tv[rows, :].astype(F32)
        sc[rows, :] = (wide * gain_ref[...]).astype(BF16)
        two = wide * wide
        acc = two[:, 0:LANES]
        for k in range(1, KT // LANES):
            acc = acc + two[:, k * LANES:(k + 1) * LANES]
        scale[rows, :] = acc
        return 0

    lax.fori_loop(0, SLAB // 64, scale_step, 0)
    row = jnp.sum(scale[...].T, axis=0, keepdims=True)
    sq[t] = jnp.concatenate([row[:, i * LANES:(i + 1) * LANES] for i in range(4)] * 2, axis=0)

    other = 1 - c
    cx = [rcopy(ctx_ref, cv.at[my_rows], core_s, core_r, fs_dev(core_peer))]
    for q in range(2):
        theirs = pl.ds(pl.multiple_of(q * HALF + other * LANES, LANES), LANES)
        cx.append(rcopy(resid_ref.at[:, theirs], rv.at[q, my_rows], core_s, core_r, fs_dev(core_peer)))

    def wo_copy(q, src, dst, lane):
        lanes = pl.ds(pl.multiple_of(q * HALF + (dst % 2) * LANES, LANES), LANES)
        return rcopy(wout_ref.at[:, lanes],
                     wv.at[pl.ds(pl.multiple_of(src * KB, KB), KB), pl.ds(q * LANES, LANES)],
                     w_s, wo_r.at[lane], fs_dev(dst))

    def wt_copy(src, dst):
        return rcopy(bw.at[dst // 2], wts.at[src],
                     wt_s, wt_r, fs_dev(dst))

    def sq_copy(src, dst):
        return rcopy(sq.at[src], sq.at[src], sq_s, sq_r, tp_dev(dst))

    def each_fs(fn):
        def body(s, _):
            fn(lax.rem(f + s, FS))
            return 0
        lax.fori_loop(1, FS, body, 0)

    def each_tp(fn):
        def body(s, _):
            fn(lax.rem(t + s, TP))
            return 0
        lax.fori_loop(1, TP, body, 0)

    wt_mine = pltpu.make_async_copy(bw.at[g], wts.at[f], my_sem.at[0])
    wt_mine.start()

    near_chips = (core_peer, 2 * xl_chip, 2 * xl_chip + 1)

    def w_rows(yy):
        return pl.ds(pl.multiple_of(yy * 4 * KB, 4 * KB), 4 * KB)

    y_up, y_dn, y_far = lax.rem(y + 1, 4), lax.rem(y + 3, 4), lax.rem(y + 2, 4)

    def y_dev(yy):
        return fs_dev(yy * 4 + xl * 2 + c)

    def y_side(up):
        return y_dev(y_up if up else y_dn)

    def wy_copy(up, rows):
        view = wv.at[rows, 0:LANES]
        return rcopy(view, view, w_s, wy_r.at[up], y_side(up))

    def wf_copy(up, yy):
        view = wv.at[pl.ds(pl.multiple_of(yy * 4 * KB + (0 if up else 2 * KB), 2 * KB), 2 * KB), 0:LANES]
        return rcopy(view, view, w_s, wf_r, y_side(up))

    def wg_copy(up, yy):
        src = yy * 4 + xl * 2 + (0 if up else 1)
        view = wv.at[pl.ds(pl.multiple_of(src * KB, KB), KB), LANES:HALF]
        return rcopy(view, view, w_s, wg_r, y_side(up))

    def wx_copy(yy, side):
        view = wv.at[pl.ds(pl.multiple_of((yy * 2 + side) * 2 * KB, 2 * KB), 2 * KB), LANES:HALF]
        return rcopy(view, view, w_s, wx_r.at[yy], fs_dev(2 * xl_chip + c))

    def y_cores(yy):
        return (yy * 4 + xl * 2, yy * 4 + xl * 2 + 1)

    def wo_stage(n):
        if n == 0:
            wo_copy(1, f, core_peer, 0).start()
            for d in y_cores(y_up):
                wo_copy(1, f, d, 1).start()
            for d in y_cores(y_dn):
                wo_copy(1, f, d, 2).start()
            for d in near_chips:
                wo_copy(0, f, d, 3).start()
        elif n == 1:
            ld_w[1].wait()
            wo_copy(1, core_peer, f, 0).wait_recv()
            wx_copy(y, xl).start()
        elif n == 2:
            ld_w[0].wait()
            arrived(wv.at[0:3 * KB, 0:LANES], wo_r.at[3])
            wy_copy(1, w_rows(y)).start()
            wy_copy(0, w_rows(y)).start()
            for up, yy in ((1, y_dn), (0, y_up)):
                arrived(wv.at[0:2 * KB, LANES:HALF], wo_r.at[2 - up])
                wg_copy(up, yy).start()
                wx_copy(yy, xl).start()
        elif n == 3:
            arrived(wv.at[0:2 * KB, LANES:HALF], wg_r)
            wx_copy(y_far, xl).start()
        else:
            wy_copy(1, w_rows(y_dn)).wait_recv()
            wf_copy(1, y_dn).start()
            wy_copy(0, w_rows(y_up)).wait_recv()
            wf_copy(0, y_up).start()

    def hidden(n):
        yy = (y, y_dn, y_up, y_far)[n]
        if n == 0:
            ld_c.wait()
            for cp in ld_r:
                cp.wait()
            arrived(cv.at[0:ROWS + ROWS * HALF // D_S], core_r)
        if n == 3:
            arrived(wv.at[0:4 * KB, 0:LANES], wf_r)
        wx_copy(yy, 1 - xl).wait_recv()

        def step(i, _):
            rows = pl.ds(pl.multiple_of(i * 512, 512), 512)
            depth = pl.ds(pl.multiple_of(yy * 4 * KB, 4 * KB), 4 * KB)
            prod = jnp.dot(cv[rows, depth], wv[w_rows(yy), :], preferred_element_type=F32)
            if n == 0:
                before = jnp.concatenate([rv[0, rows, :].astype(F32), rv[1, rows, :].astype(F32)], axis=1)
            else:
                before = hv[rows, :]
            hv[rows, :] = prod + before
            return 0

        lax.fori_loop(0, 2 * ROWS // 512, step, 0)

    def columns_of_weights():
        arrived(wts.at[0:FS - 1], wt_r)
        wt_mine.wait()

        def one(i, _):
            wcol[i] = jnp.broadcast_to(wts[i][0:1], (LANES, LANES)).T
            return 0

        lax.fori_loop(0, FS, one, 0)

    def piece(k, r, x):
        return (k * 4 + r) * 2 + x

    def z2_copy(k, up):
        return rcopy(part.at[piece(k, 0, up)], zr2.at[k, up], z_s, z2_r.at[k, up],
                     tp_dev(z_up if up else z_dn))

    def z1_copy(k, up, x):
        return rcopy(part.at[piece(k, 1 if up else 2, x)], zr1.at[k, up, x],
                     z_s, z1_r.at[k], tp_dev(z_up if up else z_dn))

    def product(q, r):
        first = (q * 4 + r) * 2
        pltpu.make_async_copy(pv.at[pl.ds(first, 2)], pv.at[pl.ds(first, 2)], pv_sem.at[q * 4 + r]).wait()

        def body(x, _):
            both = jnp.dot(sc[...], pv[(q * 4 + r) * 2 + x], preferred_element_type=F32).astype(BF16)
            part[piece(2 * q, r, x)] = both[:, :LANES]
            part[piece(2 * q + 1, r, x)] = both[:, LANES:]
            return 0

        lax.fori_loop(0, 2, body, 0)

    def z_far(k):
        z2_copy(k, 1).start()
        z2_copy(k, 0).start()

    def z_near(k, up):
        z1_copy(k, up, 1 - up).start()

    def z_middle(k):
        for up in (1, 0):
            z2_copy(k, up).wait_recv()
            u = piece(k, 1 if up else 2, up)
            part[u] = (part[u].astype(F32) + zr2[k, up].astype(F32)).astype(BF16)
            z1_copy(k, up, up).start()

    def z_total(k, x):
        return (part[piece(k, 3, x)].astype(F32) + zr1[k, 0, x].astype(F32)) + zr1[k, 1, x].astype(F32)

    def xh_copy(k):
        return rcopy(part.at[piece(k, 3, 1 - xh)], xr.at[k], z_s, xh_r.at[k], tp_dev(xh_peer))

    def z_last(k):
        arrived(zr1.at[k], z1_r.at[k])
        part[piece(k, 3, 1 - xh)] = z_total(k, 1 - xh).astype(BF16)
        xh_copy(k).start()

    def ar_copy(k, src, dst):
        return rcopy(buckets.at[k, pl.ds(pl.multiple_of((dst // 2) * 2 * CAP, 2 * CAP), 2 * CAP)],
                     arr.at[k // 2, src], ar_s, ar_r.at[k // 2], fs_dev(dst))

    def ar_mine(k):
        return pltpu.make_async_copy(
            buckets.at[k, pl.ds(pl.multiple_of(g * 2 * CAP, 2 * CAP), 2 * CAP)], arr.at[k // 2, f], my_sem.at[1 + k // 2])

    def each_owner(k, fn):
        def body(s, _):
            fn(2 * lax.rem(g + s, FS // 2) + k % 2)
            return 0

        lax.fori_loop(1, FS // 2, body, 0)

        @pl.when(c != k % 2)
        def _():
            fn(core_peer)

    def regroup(k):
        xh_copy(k).wait_recv()
        raw = z_total(k, xh) + xr[k].astype(F32)
        fitted = (raw * scale[...]).astype(BF16)
        buckets[k] = jnp.dot(onehot[...], fitted, preferred_element_type=F32).astype(BF16)
        each_owner(k, lambda d: ar_copy(k, f, d).start())

        @pl.when(c == k % 2)
        def _():
            ar_mine(k).start()

    def rs_copy(q, src, dst):
        return rcopy(pg.at[q, dst], rsv.at[q, src], rs_s, rs_r.at[2 * q + src % 2], fs_dev(dst))

    def rs_mine(q):
        return pltpu.make_async_copy(pg.at[q, f], rsv.at[q, f], my_sem.at[3 + q])

    def ry_copy(src, dst):
        return rcopy(pg.at[0, pl.ds(dst * 4, 4)], rsy.at[src], ry_s, ry_r, y_dev(dst))

    def rs_mid(k):
        @pl.when(c == k % 2)
        def _():
            arrived(rsy.at[0:3], ry_r)
            for i in range(4):
                acc = pg[0, y * 4 + i].astype(F32)
                for s in range(1, 4):
                    acc = acc + rsy[lax.rem(y + s, 4), i].astype(F32)
                pg[0, y * 4 + i] = acc.astype(BF16)
            for d in near_chips:
                rs_copy(0, f, d).start()
            rs_mine(0).start()

    def gradient(q):
        def one(s, total):
            src = lax.rem(f + s, FS)

            for j in range(2):
                rows = pl.ds(pl.multiple_of(j * ROWS + src * CAP, CAP), CAP)
                diff = hv[rows, q * LANES:(q + 1) * LANES] - arr[q, src, j * CAP:(j + 1) * CAP, :].astype(F32)
                wd = wcol[src, j * CAP:(j + 1) * CAP, :] * diff
                gv[rows, :] = wd * (2.0 / DENOM)
                terms = wd * diff
                for k in range(CAP // 8):
                    total = total + terms[k * 8:(k + 1) * 8]
            return total

        total = lb[f] if q else jnp.zeros((8, LANES), F32)
        lb[f] = lax.fori_loop(0, FS, one, total)
        if q:
            each_fs(lambda d: l1_copy(f, d).start())
        gt[...] = gv[...].T.astype(BF16)

        def term(i, _):
            dst = lax.rem((y + 2) * 4 + i, FS) if q == 0 else lax.rem(f + 1 + i, FS)
            cols = pl.ds(pl.multiple_of(dst * KB, KB), KB)
            pg[q, dst] = jnp.dot(gt[...], cv[:, cols], preferred_element_type=F32).astype(BF16)
            if q:
                @pl.when(i < FS - 1)
                def _():
                    rs_copy(q, f, dst).start()
            else:
                @pl.when((i % 4 == 3) & (dst // 4 != y))
                def _():
                    ry_copy(y, dst // 4).start()

            return 0

        if q:
            lax.fori_loop(0, FS, term, 0)
            rs_mine(q).start()
        else:
            for n in (0, 3, 1, 2):
                lax.fori_loop(4 * n, 4 * n + 4, term, 0)

    def student(k):
        @pl.when(c == k % 2)
        def _():
            ar_mine(k).wait()
            arrived(arr.at[k // 2, 0:FS - 1], ar_r.at[k // 2])
            gradient(k // 2)

    def collect(k):
        q, h = k // 2, k % 2

        count = FS // 2 if q else 2

        @pl.when(c == h)
        def _():
            rs_mine(q).wait()
            arrived(rsv.at[q, 0:count - 1], rs_r.at[k])

        @pl.when(c != h)
        def _():
            arrived(rsv.at[q, 0:count], rs_r.at[k])

        if q:
            acc = rsv[q, h].astype(F32)
            for i in range(1, FS // 2):
                acc = acc + rsv[q, 2 * i + h].astype(F32)
        else:
            acc = rsv[q, 2 * g + h].astype(F32) + rsv[q, 2 * xl_chip + h].astype(F32)
        out_ref[q * HALF + h * LANES:q * HALF + (h + 1) * LANES, :] = acc.astype(BF16)

    def l1_copy(src, dst):
        return rcopy(lb.at[src], lb.at[src], l1_s, l1_r, fs_dev(dst))

    def l2_copy(src, dst):
        return rcopy(lt.at[src], lt.at[src], l2_s, l2_r, tp_dev(dst))

    def row_scales():
        arrived(sq.at[0:TP - 1], sq_r)
        squares = sq[0]
        for i in range(1, TP):
            squares = squares + sq[i]
        rows_scale = lax.rsqrt(squares / D_T + 1e-05)
        for i in range(4):
            scale[i * LANES:(i + 1) * LANES, :] = jnp.broadcast_to(rows_scale[i:i + 1], (LANES, LANES)).T

    def loss_a():
        arrived(lb.at[0:FS - 1], l1_r)
        total = lb[0]
        for i in range(1, FS):
            total = total + lb[i]
        lt[t] = total
        each_tp(lambda d: l2_copy(t, d).start())

    def loss_b():
        arrived(lt.at[0:TP - 1], l2_r)
        total = lt[0]
        for i in range(1, TP):
            total = total + lt[i]
        total = jnp.sum(jnp.sum(total, axis=0, keepdims=True), axis=1, keepdims=True) / DENOM
        loss_ref[...] = jnp.broadcast_to(total, (8, LANES))

    product(0, 0)
    pl.semaphore_wait(barrier, FS - 1 + TP - 1)
    z_far(0)
    wo_stage(0)
    for cp in cx:
        cp.start()
    each_tp(lambda d: sq_copy(t, d).start())
    product(0, 1)
    z_near(0, 1)
    wo_stage(1)
    product(0, 2)
    z_near(0, 0)
    z_far(1)
    each_fs(lambda d: wt_copy(f, d).start())
    product(0, 3)
    z_middle(0)
    z_near(1, 1)
    z_near(1, 0)
    wo_stage(2)
    product(1, 0)
    z_far(2)
    product(1, 1)
    product(1, 2)
    z_middle(1)
    z_near(2, 1)
    z_near(2, 0)
    z_far(3)
    product(1, 3)
    row_scales()
    z_last(0)
    wo_stage(3)
    wo_stage(4)
    hidden(0)
    columns_of_weights()
    z_middle(2)
    z_near(3, 1)
    z_near(3, 0)
    regroup(0)
    z_last(1)
    hidden(1)
    hidden(2)
    z_middle(3)
    regroup(1)
    hidden(3)
    z_last(2)
    student(0)
    student(1)
    regroup(2)
    z_last(3)
    regroup(3)
    student(2)
    student(3)
    rs_mid(0)
    rs_mid(1)
    loss_a()
    collect(0)
    collect(1)
    collect(2)
    collect(3)
    loss_b()

    sent(cv.at[0:ROWS + ROWS * HALF // D_S], core_s)
    sent(wv.at[0:15 * KB], w_s)
    sent(part.at[0:28], z_s)
    sent(arr.at[:, 0:FS - 1], ar_s)
    sent(rsv.at[:, 0:9], rs_s)
    sent(pg.at[0, 0:12], ry_s)
    sent(wts.at[0:FS - 1], wt_s)
    sent(lb.at[0:FS - 1], l1_s)
    sent(lt.at[0:TP - 1], l2_s)
    sent(sq.at[0:TP - 1], sq_s)


def per_device(t_hid, teacher_gain, proj, owner, seg_ids, student_ctx, student_resid, w_out):
    dma = pltpu.SemaphoreType.DMA
    anyspace = pl.BlockSpec(memory_space=pl.ANY)
    vmem = pl.BlockSpec(memory_space=pltpu.VMEM)
    out, loss = pl.pallas_call(
        kernel,
        out_shape=(jax.ShapeDtypeStruct((COLS, KB), BF16), jax.ShapeDtypeStruct((8, LANES), F32)),
        in_specs=[anyspace, vmem, anyspace, vmem, vmem, anyspace, anyspace, anyspace],
        out_specs=(vmem, vmem),
        scratch_shapes=[
            pltpu.VMEM((SLAB, KT), BF16),
            pltpu.VMEM((SLAB, KT), BF16),
            pltpu.VMEM((16, KT, HALF), BF16),
            pltpu.VMEM((2 * ROWS, D_S), BF16),
            pltpu.VMEM((2, 2 * ROWS, LANES), BF16),
            pltpu.VMEM((D_S, HALF), BF16),
            pltpu.VMEM((32, SLAB, LANES), BF16),
            pltpu.VMEM((4, 2, SLAB, LANES), BF16),
            pltpu.VMEM((4, 2, 2, SLAB, LANES), BF16),
            pltpu.VMEM((4, SLAB, LANES), BF16),
            pltpu.VMEM((TP, 8, LANES), F32),
            pltpu.VMEM((SLAB, LANES), F32),
            pltpu.VMEM((ROWS, SLAB), BF16),
            pltpu.VMEM((4, ROWS, LANES), BF16),
            pltpu.VMEM((FS // 2, 8, LANES), F32),
            pltpu.VMEM((2, FS, 2 * CAP, LANES), BF16),
            pltpu.VMEM((FS, 8, LANES), F32),
            pltpu.VMEM((FS, LANES, LANES), F32),
            pltpu.VMEM((2 * ROWS, HALF), F32),
            pltpu.VMEM((2 * ROWS, LANES), F32),
            pltpu.VMEM((LANES, 2 * ROWS), BF16),
            pltpu.VMEM((2, FS, LANES, KB), BF16),
            pltpu.VMEM((2, FS, LANES, KB), BF16),
            pltpu.VMEM((4, 4, LANES, KB), BF16),
            pltpu.VMEM((FS, 8, LANES), F32),
            pltpu.VMEM((TP, 8, LANES), F32),
            dma((6,)), dma((8,)), dma((5,)), dma, dma, dma, dma((4,)), dma((2,)), dma, dma, dma((4,)),
            dma, dma, dma, dma, dma, dma((4, 2)), dma((4,)), dma((4,)), dma, dma((2,)), dma, dma((4,)),
            dma, dma, dma, dma, dma, dma,
        ],
        compiler_params=pltpu.CompilerParams(collective_id=0, has_side_effects=True, vmem_limit_bytes=62 << 20),
        cost_estimate=pl.CostEstimate(flops=15 * 10 ** 9, bytes_accessed=32 << 20, transcendentals=0),
    )(t_hid, teacher_gain.reshape(1, KT), proj, owner.reshape(1, SLAB), seg_ids, student_ctx, student_resid, w_out)
    return loss[0, 0], out.T


def solution(mesh):
    return jax.shard_map(
        per_device,
        mesh=mesh,
        in_specs=(
            P("fsdp", "tp"),
            P("tp"),
            P("tp", None),
            P("fsdp", None),
            P("fsdp", None),
            P("fsdp", None),
            P("fsdp", "tp"),
            P("fsdp", "tp"),
        ),
        out_specs=(P(), P("fsdp", "tp")),
        check_vma=False,
    )
```

time: 535 us -> 87.3 us (0.16)
  waiting for transfers between devices: 370 us -> 0 us
  blocking collectives: 88.3 us -> 0 us
  Pallas kernels: 0 us -> 83.5 us
  matrix products: 31.2 us -> 0 us
  between operations: 17.4 us -> 0.64 us
  starting transfers between devices: 12.2 us -> 0 us
  other arithmetic: 8.02 us -> 0 us
    psum x1 -> x0, waiting for transfers between devices: 328 us -> none  [per_device(): summed, squares_all = lax.psum((raw, squares), 'tp')]
    psum x2 -> x0, blocking collectives: 88.3 us -> none  [the longest x1 65.4 us: per_device(): loss = lax.psum(local_loss, ('tp', 'fsdp')) / denom]
    pallas_call x0 -> x1, Pallas kernels: none -> 83.5 us  [per_device(): pl.pallas_call(kernel, out_shape=(jax.ShapeDtypeStruct((COLS, KB), BF16),...]
    dot_general x3 -> x0, matrix products: 31.2 us -> none  [the longest x1 14.9 us: per_device(): raw = jnp.dot(scaled, proj, preferred_element_type=jnp.float32)]
    reduce_scatter x1 -> x0, waiting for transfers between devices: 29.9 us -> none  [per_device(): lax.psum_scatter(lax.dot_general(inputs, grad_rows, (((0,), (0,)), ((), (...]
    all_to_all x2 -> x0, starting transfers between devices: 11.9 us -> none  [the longest x1 6.91 us: per_device(): lax.all_to_all(bucket_weight, 'fsdp', split_axis=0, concat_axis=0, tiled=...]
    all_to_all x2 -> x0, waiting for transfers between devices: 11.5 us -> none  [the longest x1 11.5 us: per_device(): lax.all_to_all(buckets, 'fsdp', split_axis=0, concat_axis=0, tiled=True)]
  transfers between devices with their start and end apart: 5 -> 0, of which waited for: 3 -> 0; matrix products, arithmetic and copies ran while one was open for 2% -> 0% of each run, Pallas kernels for 0% -> 0%
where the time goes in v2:
time: 87.3 us; the launch traced here: 87.1 us
  Pallas kernels  83.5 us (96%)
  local copies, waits for them, and re-layouts  2.99 us (3%)
    pallas_call x1, Pallas kernels, per_device(): pl.pallas_call(kernel, out_shape=(jax.ShapeDtypeStruct((COLS, KB), BF16),...  83.5 us
    unnamed x1, local copies, waits for them, and re-layouts  1.79 us

profile of v2, /device:TPU:1, one launch (start us, length us, event | category | flops | bytes accessed | tf_op | source)
XLA Modules:
  0.0 87.1 jit_solution(8417739964657636029)
XLA Ops:
  0.6 83.5 %shard_map.95 = (bf16[512,256]{1,0:T(8,128)(2,1)}, f32[8,128]{1,0:T(8,128)}) custom-call(bf16[512,2048]{1,0:T(8,128)(2,1)} %t_ref.1, f32[1,2048]{1,0:T(1,128)} %bitcast.5, bf16[2048,4096]{1,0:T(8,128)(2,1)} %proj_ref.1, s32[1,512]{1,0:T(1,128)} %bitcast.6, s32[1,512]{1,0:T(1,128)} %seg_ref.1, bf16[768,4096]{1,0:T(8,128)(2,1)} %ctx_ref.1, ...), custom_call_target="tpu_custom_call" | custom-call | flops 15000000512 | bytes 33554432 | tf_op jit(solution)/shard_map/pallas_call | solution.py:549
  84.1 1.2 %slice.3 = f32[1,1]{1,0:T(1,128)} slice(f32[8,128]{1,0:T(8,128)} %get-tuple-element.4), slice={[0:1], [0:1]} | slice | bytes 8 | tf_op jit(solution)/shard_map/slice | solution.py:588
  85.3 1.8 %copy.10 = bf16[256,512]{1,0:T(8,128)(2,1)} copy(bf16[256,512]{0,1:T(8,128)(2,1)} %bitcast.4) | data formatting | bytes 524288

commit v3 on v2

--- a/solution.py
+++ b/solution.py
@@ -27,9 +27,9 @@
 def kernel(t_ref, gain_ref, proj_ref, own_ref, seg_ref, ctx_ref, resid_ref, wout_ref,
            out_ref, loss_ref,
            tv, sc, pv, cv, rv, wv, part, zr2, zr1, xr, sq, scale, onehot, buckets, bw, arr, wts, wcol,
-           hv, gv, gt, pg, rsv, rsy, lb, lt,
+           hv, gv, gt, pg, rsv, rsf, rsy, lb, lt,
            ld_sem, pv_sem, my_sem, core_s, core_r, w_s, wo_r, wy_r, wf_r, wg_r, wx_r, wt_s, wt_r, sq_s, sq_r,
-           z_s, z2_r, z1_r, xh_r, ar_s, ar_r, rs_s, rs_r, ry_s, ry_r, l1_s, l1_r, l2_s, l2_r):
+           z_s, z2_r, z1_r, xh_r, ar_s, ar_r, rs_s, rs_r, rf_r, ry_s, ry_r, l1_s, l1_r, l2_s, l2_r):
     t = lax.axis_index("tp")
     f = lax.axis_index("fsdp")
     z, xh = t // 2, t % 2
@@ -216,14 +216,14 @@
             wo_copy(1, core_peer, f, 0).wait_recv()
             wx_copy(y, xl).start()
         elif n == 2:
+            for up, yy in ((1, y_dn), (0, y_up)):
+                arrived(wv.at[0:2 * KB, LANES:HALF], wo_r.at[2 - up])
+                wg_copy(up, yy).start()
+                wx_copy(yy, xl).start()
             ld_w[0].wait()
             arrived(wv.at[0:3 * KB, 0:LANES], wo_r.at[3])
             wy_copy(1, w_rows(y)).start()
             wy_copy(0, w_rows(y)).start()
-            for up, yy in ((1, y_dn), (0, y_up)):
-                arrived(wv.at[0:2 * KB, LANES:HALF], wo_r.at[2 - up])
-                wg_copy(up, yy).start()
-                wx_copy(yy, xl).start()
         elif n == 3:
             arrived(wv.at[0:2 * KB, LANES:HALF], wg_r)
             wx_copy(y_far, xl).start()
@@ -346,80 +346,102 @@
             ar_mine(k).start()
 
     def rs_copy(q, src, dst):
-        return rcopy(pg.at[q, dst], rsv.at[q, src], rs_s, rs_r.at[2 * q + src % 2], fs_dev(dst))
+        return rcopy(pg.at[q, dst], rsv.at[q, src], rs_s.at[q], rs_r.at[2 * q + src % 2], fs_dev(dst))
 
     def rs_mine(q):
         return pltpu.make_async_copy(pg.at[q, f], rsv.at[q, f], my_sem.at[3 + q])
 
-    def ry_copy(src, dst):
-        return rcopy(pg.at[0, pl.ds(dst * 4, 4)], rsy.at[src], ry_s, ry_r, y_dev(dst))
+    def pair(yy, side):
+        return pl.ds(pl.multiple_of(yy * 4 + side * 2, 2), 2)
+
+    def rf_copy(q, up):
+        return rcopy(pg.at[q, pair(y_far, 1 - up)], rsf.at[q, up], ry_s.at[q], rf_r.at[q, up], y_side(up))
+
+    def ry_copy(q, up, side):
+        return rcopy(pg.at[q, pair(y_up if up else y_dn, side)], rsy.at[q, up, pl.ds(side * 2, 2)],
+                     ry_s.at[q], ry_r.at[q], y_side(up))
+
+    def rs_ring(k):
+        @pl.when(c == k % 2)
+        def _():
+            q = k // 2
+            for up in (1, 0):
+                rf_copy(q, up).wait_recv()
+                for i in range(2):
+                    at = (y_up if up else y_dn) * 4 + (1 - up) * 2 + i
+                    pg[q, at] = (pg[q, at].astype(F32) + rsf[q, up, i].astype(F32)).astype(BF16)
+                ry_copy(q, up, 1 - up).start()
 
     def rs_mid(k):
         @pl.when(c == k % 2)
         def _():
-            arrived(rsy.at[0:3], ry_r)
+            q = k // 2
+            arrived(rsy.at[q], ry_r.at[q])
             for i in range(4):
-                acc = pg[0, y * 4 + i].astype(F32)
-                for s in range(1, 4):
-                    acc = acc + rsy[lax.rem(y + s, 4), i].astype(F32)
-                pg[0, y * 4 + i] = acc.astype(BF16)
+                acc = pg[q, y * 4 + i].astype(F32) + rsy[q, 0, i].astype(F32) + rsy[q, 1, i].astype(F32)
+                pg[q, y * 4 + i] = acc.astype(BF16)
             for d in near_chips:
-                rs_copy(0, f, d).start()
-            rs_mine(0).start()
-
-    def gradient(q):
+                rs_copy(q, f, d).start()
+            rs_mine(q).start()
+
+    def gradient(k, part_of):
+        q = k // 2
+
         def one(s, total):
             src = lax.rem(f + s, FS)
-
             for j in range(2):
                 rows = pl.ds(pl.multiple_of(j * ROWS + src * CAP, CAP), CAP)
                 diff = hv[rows, q * LANES:(q + 1) * LANES] - arr[q, src, j * CAP:(j + 1) * CAP, :].astype(F32)
                 wd = wcol[src, j * CAP:(j + 1) * CAP, :] * diff
                 gv[rows, :] = wd * (2.0 / DENOM)
-                terms = wd * diff
-                for k in range(CAP // 8):
-                    total = total + terms[k * 8:(k + 1) * 8]
+                errors = wd * diff
+                for i in range(CAP // 8):
+                    total = total + errors[i * 8:(i + 1) * 8]
             return total
 
-        total = lb[f] if q else jnp.zeros((8, LANES), F32)
-        lb[f] = lax.fori_loop(0, FS, one, total)
-        if q:
-            each_fs(lambda d: l1_copy(f, d).start())
-        gt[...] = gv[...].T.astype(BF16)
-
-        def term(i, _):
-            dst = lax.rem((y + 2) * 4 + i, FS) if q == 0 else lax.rem(f + 1 + i, FS)
+        if part_of != 1:
+            total = lb[f] if q else jnp.zeros((8, LANES), F32)
+            lb[f] = lax.fori_loop(0, FS, one, total)
+            if q:
+                each_fs(lambda d: l1_copy(f, d).start())
+            gt[...] = gv[...].T.astype(BF16)
+
+        def term(dst):
             cols = pl.ds(pl.multiple_of(dst * KB, KB), KB)
             pg[q, dst] = jnp.dot(gt[...], cv[:, cols], preferred_element_type=F32).astype(BF16)
-            if q:
-                @pl.when(i < FS - 1)
-                def _():
-                    rs_copy(q, f, dst).start()
-            else:
-                @pl.when((i % 4 == 3) & (dst // 4 != y))
-                def _():
-                    ry_copy(y, dst // 4).start()
-
-            return 0
-
-        if q:
-            lax.fori_loop(0, FS, term, 0)
-            rs_mine(q).start()
-        else:
-            for n in (0, 3, 1, 2):
-                lax.fori_loop(4 * n, 4 * n + 4, term, 0)
-
-    def student(k):
+
+        def terms(yy, side):
+            def one(i, _):
+                term(yy * 4 + side * 2 + i)
+                return 0
+
+            lax.fori_loop(0, 2, one, 0)
+
+        if part_of != 1:
+            for up in (1, 0):
+                terms(y_far, 1 - up)
+                rf_copy(q, up).start()
+            for up in (1, 0):
+                terms(y_up if up else y_dn, up)
+                ry_copy(q, up, up).start()
+        if part_of != 0:
+            for up in (1, 0):
+                terms(y_up if up else y_dn, 1 - up)
+            for side in range(2):
+                terms(y, side)
+
+    def student(k, part_of=2):
         @pl.when(c == k % 2)
         def _():
-            ar_mine(k).wait()
-            arrived(arr.at[k // 2, 0:FS - 1], ar_r.at[k // 2])
-            gradient(k // 2)
+            if part_of != 1:
+                ar_mine(k).wait()
+                arrived(arr.at[k // 2, 0:FS - 1], ar_r.at[k // 2])
+            gradient(k, part_of)
 
     def collect(k):
         q, h = k // 2, k % 2
 
-        count = FS // 2 if q else 2
+        count = 2
 
         @pl.when(c == h)
         def _():
@@ -430,12 +452,7 @@
         def _():
             arrived(rsv.at[q, 0:count], rs_r.at[k])
 
-        if q:
-            acc = rsv[q, h].astype(F32)
-            for i in range(1, FS // 2):
-                acc = acc + rsv[q, 2 * i + h].astype(F32)
-        else:
-            acc = rsv[q, 2 * g + h].astype(F32) + rsv[q, 2 * xl_chip + h].astype(F32)
+        acc = rsv[q, 2 * g + h].astype(F32) + rsv[q, 2 * xl_chip + h].astype(F32)
         out_ref[q * HALF + h * LANES:q * HALF + (h + 1) * LANES, :] = acc.astype(BF16)
 
     def l1_copy(src, dst):
@@ -484,48 +501,56 @@
     z_far(1)
     each_fs(lambda d: wt_copy(f, d).start())
     product(0, 3)
+    product(1, 0)
     z_middle(0)
     z_near(1, 1)
     z_near(1, 0)
     wo_stage(2)
-    product(1, 0)
-    z_far(2)
     product(1, 1)
     product(1, 2)
+    z_far(2)
+    product(1, 3)
+    row_scales()
+    wo_stage(3)
     z_middle(1)
     z_near(2, 1)
     z_near(2, 0)
     z_far(3)
-    product(1, 3)
-    row_scales()
+    columns_of_weights()
     z_last(0)
-    wo_stage(3)
+    hidden(0)
     wo_stage(4)
-    hidden(0)
-    columns_of_weights()
+    hidden(1)
+    hidden(2)
+    regroup(0)
     z_middle(2)
     z_near(3, 1)
     z_near(3, 0)
-    regroup(0)
     z_last(1)
-    hidden(1)
-    hidden(2)
+    hidden(3)
+    student(0, 0)
     z_middle(3)
     regroup(1)
-    hidden(3)
     z_last(2)
-    student(0)
-    student(1)
+    student(0, 1)
+    rs_ring(0)
+    z_last(3)
     regroup(2)
-    z_last(3)
+    student(1, 0)
+    rs_mid(0)
     regroup(3)
+    student(1, 1)
+    rs_ring(1)
     student(2)
+    rs_ring(2)
     student(3)
-    rs_mid(0)
+    loss_a()
     rs_mid(1)
-    loss_a()
+    rs_ring(3)
+    rs_mid(2)
     collect(0)
     collect(1)
+    rs_mid(3)
     collect(2)
     collect(3)
     loss_b()
@@ -534,8 +559,9 @@
     sent(wv.at[0:15 * KB], w_s)
     sent(part.at[0:28], z_s)
     sent(arr.at[:, 0:FS - 1], ar_s)
-    sent(rsv.at[:, 0:9], rs_s)
-    sent(pg.at[0, 0:12], ry_s)
+    for q in range(2):
+        sent(rsv.at[0, 0:3], rs_s.at[q])
+        sent(pg.at[0, 0:12], ry_s.at[q])
     sent(wts.at[0:FS - 1], wt_s)
     sent(lb.at[0:FS - 1], l1_s)
     sent(lt.at[0:TP - 1], l2_s)
@@ -575,12 +601,13 @@
             pltpu.VMEM((LANES, 2 * ROWS), BF16),
             pltpu.VMEM((2, FS, LANES, KB), BF16),
             pltpu.VMEM((2, FS, LANES, KB), BF16),
-            pltpu.VMEM((4, 4, LANES, KB), BF16),
+            pltpu.VMEM((2, 2, 2, LANES, KB), BF16),
+            pltpu.VMEM((2, 2, 4, LANES, KB), BF16),
             pltpu.VMEM((FS, 8, LANES), F32),
             pltpu.VMEM((TP, 8, LANES), F32),
             dma((6,)), dma((8,)), dma((5,)), dma, dma, dma, dma((4,)), dma((2,)), dma, dma, dma((4,)),
-            dma, dma, dma, dma, dma, dma((4, 2)), dma((4,)), dma((4,)), dma, dma((2,)), dma, dma((4,)),
-            dma, dma, dma, dma, dma, dma,
+            dma, dma, dma, dma, dma, dma((4, 2)), dma((4,)), dma((4,)), dma, dma((2,)), dma((2,)), dma((4,)),
+            dma((2, 2)), dma((2,)), dma((2,)), dma, dma, dma, dma,
         ],
         compiler_params=pltpu.CompilerParams(collective_id=0, has_side_effects=True, vmem_limit_bytes=62 << 20),
         cost_estimate=pl.CostEstimate(flops=15 * 10 ** 9, bytes_accessed=32 << 20, transcendentals=0),

time: 87.3 us -> 76.3 us (0.87)
  Pallas kernels: 83.5 us -> 72.5 us
    pallas_call x1, Pallas kernels: 83.5 us -> 72.5 us  [per_device(): pl.pallas_call(kernel, out_shape=(jax.ShapeDtypeStruct((COLS, KB), BF16),...]
where the time goes in v3:
time: 76.3 us; the launch traced here: 76.1 us
  Pallas kernels  72.5 us (95%)
  local copies, waits for them, and re-layouts  2.99 us (4%)
    pallas_call x1, Pallas kernels, per_device(): pl.pallas_call(kernel, out_shape=(jax.ShapeDtypeStruct((COLS, KB), BF16),...  72.5 us
    unnamed x1, local copies, waits for them, and re-layouts  1.79 us

profile of v3, /device:TPU:1, one launch (start us, length us, event | category | flops | bytes accessed | tf_op | source)
XLA Modules:
  0.0 76.1 jit_solution(6900621803883855233)
XLA Ops:
  0.6 72.5 %shard_map.95 = (bf16[512,256]{1,0:T(8,128)(2,1)}, f32[8,128]{1,0:T(8,128)}) custom-call(bf16[512,2048]{1,0:T(8,128)(2,1)} %t_ref.1, f32[1,2048]{1,0:T(1,128)} %bitcast.5, bf16[2048,4096]{1,0:T(8,128)(2,1)} %proj_ref.1, s32[1,512]{1,0:T(1,128)} %bitcast.6, s32[1,512]{1,0:T(1,128)} %seg_ref.1, bf16[768,4096]{1,0:T(8,128)(2,1)} %ctx_ref.1, ...), custom_call_target="tpu_custom_call" | custom-call | flops 15000000512 | bytes 33554432 | tf_op jit(solution)/shard_map/pallas_call | solution.py:575
  73.1 1.2 %slice.3 = f32[1,1]{1,0:T(1,128)} slice(f32[8,128]{1,0:T(8,128)} %get-tuple-element.4), slice={[0:1], [0:1]} | slice | bytes 8 | tf_op jit(solution)/shard_map/slice | solution.py:615
  74.3 1.8 %copy.10 = bf16[256,512]{1,0:T(8,128)(2,1)} copy(bf16[256,512]{0,1:T(8,128)(2,1)} %bitcast.4) | data formatting | bytes 524288

commit v4 on v3

--- a/solution.py
+++ b/solution.py
@@ -28,8 +28,14 @@
            out_ref, loss_ref,
            tv, sc, pv, cv, rv, wv, part, zr2, zr1, xr, sq, scale, onehot, buckets, bw, arr, wts, wcol,
            hv, gv, gt, pg, rsv, rsf, rsy, lb, lt,
-           ld_sem, pv_sem, my_sem, core_s, core_r, w_s, wo_r, wy_r, wf_r, wg_r, wx_r, wt_s, wt_r, sq_s, sq_r,
+           t_sem, ld_sem, pv_sem, my_sem, core_s, core_r, w_s, wo_r, wy_r, wf_r, wg_r, wx_r, wt_s, wt_r, sq_s, sq_r,
            z_s, z2_r, z1_r, xh_r, ar_s, ar_r, rs_s, rs_r, rf_r, ry_s, ry_r, l1_s, l1_r, l2_s, l2_r):
+    def t_rows(i):
+        rows = pl.ds(i * SLAB // 4, SLAB // 4)
+        return pltpu.make_async_copy(t_ref.at[rows], tv.at[rows], t_sem.at[i])
+
+    for i in range(4):
+        t_rows(i).start()
     t = lax.axis_index("tp")
     f = lax.axis_index("fsdp")
     z, xh = t // 2, t % 2
@@ -70,8 +76,6 @@
     lax.fori_loop(1, FS, greet_fs, 0)
     lax.fori_loop(1, TP, greet_tp, 0)
 
-    ld_t = pltpu.make_async_copy(t_ref, tv, ld_sem.at[0])
-    ld_t.start()
     rels = (2, 1, 3, 0)
 
     def unit_copy(q, r, x):
@@ -91,35 +95,6 @@
         ld_w.append(pltpu.make_async_copy(
             wout_ref.at[:, mine], wv.at[pl.ds(pl.multiple_of(f * KB, KB), KB), pl.ds(q * LANES, LANES)],
             ld_sem.at[4 + q]))
-    own = own_ref[...]
-    seg = seg_ref[...]
-    marks = (lax.broadcasted_iota(jnp.int32, (FS, SLAB), 0) == own)
-    earlier = (lax.broadcasted_iota(jnp.int32, (SLAB, SLAB), 0)
-               < lax.broadcasted_iota(jnp.int32, (SLAB, SLAB), 1)).astype(F32).astype(BF16)
-    marks = marks.astype(F32)
-    before = jnp.dot(marks.astype(BF16), earlier, preferred_element_type=F32)
-    rank = jnp.sum(before * marks, axis=0, keepdims=True).astype(jnp.int32)
-    slot = own * CAP + rank
-    onehot[...] = (lax.broadcasted_iota(jnp.int32, (ROWS, SLAB), 0) == slot).astype(F32).astype(BF16)
-    member = (lax.broadcasted_iota(jnp.int32, (SEGS, SLAB), 0) == seg).astype(F32)
-    counts = jnp.sum(member, axis=1, keepdims=True)
-    length = jnp.sum(member * counts, axis=0, keepdims=True)
-    weight = jnp.broadcast_to((1.0 / length).astype(BF16), (16, SLAB))
-    wide_slot = (own // 2) * LANES + (own % 2) * CAP + rank
-    spread = (lax.broadcasted_iota(jnp.int32, (FS // 2 * LANES, SLAB), 0) == wide_slot).astype(F32).astype(BF16)
-    moved = lax.dot_general(weight, spread, (((1,), (1,)), ((), ())), preferred_element_type=F32)
-    for i in range(FS // 2):
-        bw[i] = moved[0:8, i * LANES:(i + 1) * LANES]
-
-    ld_t.wait()
-    for q in range(2):
-        for r in range(4):
-            for x in range(2):
-                if q or r:
-                    unit_copy(q, r, x).start()
-    for cp in ld_w + ld_r + [ld_c]:
-        cp.start()
-
     def scale_step(i, _):
         rows = pl.ds(pl.multiple_of(i * 64, 64), 64)
         wide = tv[rows, :].astype(F32)
@@ -131,7 +106,17 @@
         scale[rows, :] = acc
         return 0
 
-    lax.fori_loop(0, SLAB // 64, scale_step, 0)
+    for i in range(4):
+        t_rows(i).wait()
+        if i == 3:
+            for q in range(2):
+                for r in range(4):
+                    for x in range(2):
+                        if q or r:
+                            unit_copy(q, r, x).start()
+            for cp in ld_w + ld_r + [ld_c]:
+                cp.start()
+        lax.fori_loop(2 * i, 2 * i + 2, scale_step, 0)
     row = jnp.sum(scale[...].T, axis=0, keepdims=True)
     sq[t] = jnp.concatenate([row[:, i * LANES:(i + 1) * LANES] for i in range(4)] * 2, axis=0)
 
@@ -167,7 +152,6 @@
         lax.fori_loop(1, TP, body, 0)
 
     wt_mine = pltpu.make_async_copy(bw.at[g], wts.at[f], my_sem.at[0])
-    wt_mine.start()
 
     near_chips = (core_peer, 2 * xl_chip, 2 * xl_chip + 1)
 
@@ -453,13 +437,35 @@
             arrived(rsv.at[q, 0:count], rs_r.at[k])
 
         acc = rsv[q, 2 * g + h].astype(F32) + rsv[q, 2 * xl_chip + h].astype(F32)
-        out_ref[q * HALF + h * LANES:q * HALF + (h + 1) * LANES, :] = acc.astype(BF16)
+        out_ref[:, q * HALF + h * LANES:q * HALF + (h + 1) * LANES] = acc.T.astype(BF16)
 
     def l1_copy(src, dst):
         return rcopy(lb.at[src], lb.at[src], l1_s, l1_r, fs_dev(dst))
 
     def l2_copy(src, dst):
         return rcopy(lt.at[src], lt.at[src], l2_s, l2_r, tp_dev(dst))
+
+    def slots():
+        own = own_ref[...]
+        seg = seg_ref[...]
+        marks = (lax.broadcasted_iota(jnp.int32, (FS, SLAB), 0) == own)
+        earlier = (lax.broadcasted_iota(jnp.int32, (SLAB, SLAB), 0)
+                   < lax.broadcasted_iota(jnp.int32, (SLAB, SLAB), 1)).astype(F32).astype(BF16)
+        marks = marks.astype(F32)
+        before = jnp.dot(marks.astype(BF16), earlier, preferred_element_type=F32)
+        rank = jnp.sum(before * marks, axis=0, keepdims=True).astype(jnp.int32)
+        slot = own * CAP + rank
+        onehot[...] = (lax.broadcasted_iota(jnp.int32, (ROWS, SLAB), 0) == slot).astype(F32).astype(BF16)
+        member = (lax.broadcasted_iota(jnp.int32, (SEGS, SLAB), 0) == seg).astype(F32)
+        counts = jnp.sum(member, axis=1, keepdims=True)
+        length = jnp.sum(member * counts, axis=0, keepdims=True)
+        weight = jnp.broadcast_to((1.0 / length).astype(BF16), (16, SLAB))
+        wide_slot = (own // 2) * LANES + (own % 2) * CAP + rank
+        spread = (lax.broadcasted_iota(jnp.int32, (FS // 2 * LANES, SLAB), 0) == wide_slot).astype(F32).astype(BF16)
+        moved = lax.dot_general(weight, spread, (((1,), (1,)), ((), ())), preferred_element_type=F32)
+        for i in range(FS // 2):
+            bw[i] = moved[0:8, i * LANES:(i + 1) * LANES]
+        wt_mine.start()
 
     def row_scales():
         arrived(sq.at[0:TP - 1], sq_r)
@@ -484,7 +490,7 @@
         for i in range(1, TP):
             total = total + lt[i]
         total = jnp.sum(jnp.sum(total, axis=0, keepdims=True), axis=1, keepdims=True) / DENOM
-        loss_ref[...] = jnp.broadcast_to(total, (8, LANES))
+        loss_ref[...] = total
 
     product(0, 0)
     pl.semaphore_wait(barrier, FS - 1 + TP - 1)
@@ -499,7 +505,6 @@
     product(0, 2)
     z_near(0, 0)
     z_far(1)
-    each_fs(lambda d: wt_copy(f, d).start())
     product(0, 3)
     product(1, 0)
     z_middle(0)
@@ -510,13 +515,14 @@
     product(1, 2)
     z_far(2)
     product(1, 3)
+    slots()
+    each_fs(lambda d: wt_copy(f, d).start())
     row_scales()
     wo_stage(3)
     z_middle(1)
     z_near(2, 1)
     z_near(2, 0)
     z_far(3)
-    columns_of_weights()
     z_last(0)
     hidden(0)
     wo_stage(4)
@@ -528,6 +534,7 @@
     z_near(3, 0)
     z_last(1)
     hidden(3)
+    columns_of_weights()
     student(0, 0)
     z_middle(3)
     regroup(1)
@@ -537,11 +544,11 @@
     z_last(3)
     regroup(2)
     student(1, 0)
-    rs_mid(0)
     regroup(3)
     student(1, 1)
     rs_ring(1)
     student(2)
+    rs_mid(0)
     rs_ring(2)
     student(3)
     loss_a()
@@ -574,7 +581,7 @@
     vmem = pl.BlockSpec(memory_space=pltpu.VMEM)
     out, loss = pl.pallas_call(
         kernel,
-        out_shape=(jax.ShapeDtypeStruct((COLS, KB), BF16), jax.ShapeDtypeStruct((8, LANES), F32)),
+        out_shape=(jax.ShapeDtypeStruct((KB, COLS), BF16), jax.ShapeDtypeStruct((1, 1), F32)),
         in_specs=[anyspace, vmem, anyspace, vmem, vmem, anyspace, anyspace, anyspace],
         out_specs=(vmem, vmem),
         scratch_shapes=[
@@ -605,14 +612,14 @@
             pltpu.VMEM((2, 2, 4, LANES, KB), BF16),
             pltpu.VMEM((FS, 8, LANES), F32),
             pltpu.VMEM((TP, 8, LANES), F32),
-            dma((6,)), dma((8,)), dma((5,)), dma, dma, dma, dma((4,)), dma((2,)), dma, dma, dma((4,)),
+            dma((4,)), dma((6,)), dma((8,)), dma((5,)), dma, dma, dma, dma((4,)), dma((2,)), dma, dma, dma((4,)),
             dma, dma, dma, dma, dma, dma((4, 2)), dma((4,)), dma((4,)), dma, dma((2,)), dma((2,)), dma((4,)),
             dma((2, 2)), dma((2,)), dma((2,)), dma, dma, dma, dma,
         ],
         compiler_params=pltpu.CompilerParams(collective_id=0, has_side_effects=True, vmem_limit_bytes=62 << 20),
         cost_estimate=pl.CostEstimate(flops=15 * 10 ** 9, bytes_accessed=32 << 20, transcendentals=0),
     )(t_hid, teacher_gain.reshape(1, KT), proj, owner.reshape(1, SLAB), seg_ids, student_ctx, student_resid, w_out)
-    return loss[0, 0], out.T
+    return loss.reshape(()), out
 
 
 def solution(mesh):

time: 76.3 us -> 76.1 us (level)
  between operations: 0.64 us -> 2.4 us
  local copies, waits for them, and re-layouts: 2.99 us -> 1.67 us
    slice x1 -> x0, local copies, waits for them, and re-layouts: 1.2 us -> none  [per_device(): return (loss[0, 0], out.T)]
where the time goes in v4:
time: 76.1 us; the launch traced here: 75.9 us
  Pallas kernels  71.8 us (94%)
  between operations  2.4 us (3%)
  local copies, waits for them, and re-layouts  1.67 us (2%)
    pallas_call x1, Pallas kernels, per_device(): pl.pallas_call(kernel, out_shape=(jax.ShapeDtypeStruct((KB, COLS), BF16),...  71.8 us
    unnamed x1, local copies, waits for them, and re-layouts  1.67 us

profile of v4, /device:TPU:1, one launch (start us, length us, event | category | flops | bytes accessed | tf_op | source)
XLA Modules:
  0.0 75.9 jit_solution(357596301302591933)
XLA Ops:
  0.6 71.8 %shard_map.95 = (bf16[256,512]{1,0:T(8,128)(2,1)}, f32[1,1]{1,0:T(1,128)}) custom-call(bf16[512,2048]{1,0:T(8,128)(2,1)} %t_ref.1, f32[1,2048]{1,0:T(1,128)} %bitcast.3, bf16[2048,4096]{1,0:T(8,128)(2,1)} %proj_ref.1, s32[1,512]{1,0:T(1,128)} %bitcast.4, s32[1,512]{1,0:T(1,128)} %seg_ref.1, bf16[768,4096]{1,0:T(8,128)(2,1)} %ctx_ref.1, ...), custom_call_target="tpu_custom_call" | custom-call | flops 15000000512 | bytes 33554432 | tf_op jit(solution)/shard_map/pallas_call | solution.py:582
  73.1 1.7 %copy.13 = bf16[256,512]{1,0:T(8,128)(2,1)} copy(bf16[256,512]{1,0:T(8,128)(2,1)} %get-tuple-element.9) | data formatting | bytes 524288

commit v5 on v3

--- a/solution.py
+++ b/solution.py
@@ -406,16 +406,12 @@
                 each_fs(lambda d: l1_copy(f, d).start())
             gt[...] = gv[...].T.astype(BF16)
 
-        def term(dst):
-            cols = pl.ds(pl.multiple_of(dst * KB, KB), KB)
-            pg[q, dst] = jnp.dot(gt[...], cv[:, cols], preferred_element_type=F32).astype(BF16)
-
         def terms(yy, side):
-            def one(i, _):
-                term(yy * 4 + side * 2 + i)
-                return 0
-
-            lax.fori_loop(0, 2, one, 0)
+            first = yy * 4 + side * 2
+            cols = pl.ds(pl.multiple_of(first * KB, 2 * KB), 2 * KB)
+            both = jnp.dot(gt[...], cv[:, cols], preferred_element_type=F32).astype(BF16)
+            pg[q, first] = both[:, :KB]
+            pg[q, first + 1] = both[:, KB:]
 
         if part_of != 1:
             for up in (1, 0):

time: 76.3 us -> 76.1 us (level)
  no operation moved by 1% of the time
where the time goes in v5:
time: 76.1 us; the launch traced here: 75.9 us
  Pallas kernels  72.3 us (95%)
  local copies, waits for them, and re-layouts  2.99 us (4%)
    pallas_call x1, Pallas kernels, per_device(): pl.pallas_call(kernel, out_shape=(jax.ShapeDtypeStruct((COLS, KB), BF16),...  72.3 us
    unnamed x1, local copies, waits for them, and re-layouts  1.79 us

profile of v5, /device:TPU:1, one launch (start us, length us, event | category | flops | bytes accessed | tf_op | source)
XLA Modules:
  0.0 75.9 jit_solution(14962514989169087812)
XLA Ops:
  0.6 72.3 %shard_map.95 = (bf16[512,256]{1,0:T(8,128)(2,1)}, f32[8,128]{1,0:T(8,128)}) custom-call(bf16[512,2048]{1,0:T(8,128)(2,1)} %t_ref.1, f32[1,2048]{1,0:T(1,128)} %bitcast.5, bf16[2048,4096]{1,0:T(8,128)(2,1)} %proj_ref.1, s32[1,512]{1,0:T(1,128)} %bitcast.6, s32[1,512]{1,0:T(1,128)} %seg_ref.1, bf16[768,4096]{1,0:T(8,128)(2,1)} %ctx_ref.1, ...), custom_call_target="tpu_custom_call" | custom-call | flops 15000000512 | bytes 33554432 | tf_op jit(solution)/shard_map/pallas_call | solution.py:571
  72.9 1.2 %slice.3 = f32[1,1]{1,0:T(1,128)} slice(f32[8,128]{1,0:T(8,128)} %get-tuple-element.4), slice={[0:1], [0:1]} | slice | bytes 8 | tf_op jit(solution)/shard_map/slice | solution.py:611
  74.1 1.8 %copy.10 = bf16[256,512]{1,0:T(8,128)(2,1)} copy(bf16[256,512]{0,1:T(8,128)(2,1)} %bitcast.4) | data formatting | bytes 524288
